TPU v7x, 32 devices: a whole 2x2x4 slice. The times are simulated.
32 devices in a mesh: row: 8 (over y, x, core), col: 4 (over z).
Axes of the slice: x: 2, y: 2, z: 4, core: 2. Of those that a mesh axis runs over, the one named last changes fastest.
Arguments:
- tokens: bfloat16 [4096, 6144], P('row', 'col'), may hold values from -6 to 6
- gate_weight: bfloat16 [6144, 12288], P('row', 'col'), may hold values from -0.078125 to 0.078125
- up_weight: bfloat16 [6144, 12288], P('row', 'col'), may hold values from -0.078125 to 0.078125
Outputs:
- hidden: float32 [4096, 12288], P('row', 'col')
All inputs are finite; a program needn't handle non-finite values.
Results may differ from a plain program's by a relative error of at most 0.0003.
Values may be sent and summed in bfloat16 or wider, within the bound.
A program may use at most 192 MiB of HBM per device.

v0:
```python
import jax
import jax.numpy as jnp
from jax import lax
from jax.sharding import PartitionSpec as P


def accumulate(gathered, weight_rows):
    return jnp.dot(gathered, weight_rows, preferred_element_type=jnp.float32)


def per_device(tokens, gate_weight, up_weight):
    gathered = lax.all_gather(tokens, "col", axis=1, tiled=True)

    def add_single(weight_rows):
        return accumulate(gathered, weight_rows)

    gate_sum = add_single(lax.all_gather(gate_weight, "row", axis=0, tiled=True))
    up_sum = add_single(lax.all_gather(up_weight, "row", axis=0, tiled=True))
    return jax.nn.silu(gate_sum) * up_sum


def solution(mesh):
    in_specs = (P("row", "col"), P("row", "col"), P("row", "col"))
    out_specs = P("row", "col")
    return jax.shard_map(
        per_device, mesh=mesh, in_specs=in_specs, out_specs=out_specs, check_vma=False
    )
```

profile of v0, /device:TPU:0, one launch (start us, length us, event | category | flops | bytes accessed | tf_op | source)
XLA Modules:
  0.0 523.4 jit_solution(15334659808473914694)
XLA Ops:
  6.5 0.0 all-gather.4.cloned.1.call-start
  6.5 0.7 all-gather.4.cloned.1.call-update
  7.3 0.0 all-gather.6.cloned.1.call-start
  7.3 0.7 all-gather.6.cloned.1.call-update
  8.0 0.0 all-gather.8.cloned.1.call-start
  8.1 0.7 all-gather.8.cloned.1.call-update
  8.7 118.3 %all-gather.4.cloned.1.call-done = bf16[512,6144]{1,0:T(8,128)(2,1)} async-done(((bf16[512,1536]{1,0:T(8,128)(2,1)}), bf16[512,6144]{1,0:T(8,128)(2,1)}) %all-gather.4.cloned.1.call-update) | async-done | bytes 6291472 | tf_op jit(solution)/shard_map/all_gather | solution.py:12
  127.0 179.7 %all-gather.6.cloned.1.call-done = bf16[6144,3072]{1,0:T(8,128)(2,1)} async-done(((bf16[768,3072]{1,0:T(8,128)(2,1)}), bf16[6144,3072]{1,0:T(8,128)(2,1)}) %all-gather.6.cloned.1.call-update) | async-done | bytes 37748752 | tf_op jit(solution)/shard_map/all_gather | solution.py:17
  306.7 27.4 %fusion = f32[512,3072]{1,0:T(8,128)} fusion(bf16[512,6144]{1,0:T(8,128)(2,1)} %all-gather.4.cloned.1.call-done, bf16[6144,3072]{1,0:T(8,128)(2,1)} %all-gather.6.cloned.1.call-done), kind=kOutput, calls=%fused_computation.1 | convolution fusion | flops 19327352832 | bytes 50331648 | tf_op jit(solution)/shard_map/dot_general | solution.py:8
  334.1 154.2 %all-gather.8.cloned.1.call-done = bf16[6144,3072]{1,0:T(8,128)(2,1)} async-done(((bf16[768,3072]{1,0:T(8,128)(2,1)}), bf16[6144,3072]{1,0:T(8,128)(2,1)}) %all-gather.8.cloned.1.call-update) | async-done | bytes 37748752 | tf_op jit(solution)/shard_map/all_gather | solution.py:18
  488.3 28.6 %multiply_multiply_fusion = f32[512,3072]{1,0:T(8,128)} fusion(f32[512,3072]{1,0:T(8,128)} %fusion, bf16[512,6144]{1,0:T(8,128)(2,1)} %all-gather.4.cloned.1.call-done, bf16[6144,3072]{1,0:T(8,128)(2,1)} %all-gather.8.cloned.1.call-done), kind=kOutput, calls=%fused_computation | convolution fusion | flops 19335217152 | bytes 56623104 | tf_op jit(solution)/shard_map/dot_general | solution.py:8
Async XLA Ops:
  6.5 120.5 %all-gather.4.cloned.1.call-start = ((), (), s32[]{:S(2)}) async-start(), calls=%async_computation | async-start | bytes 7864320 | tf_op jit(solution)/shard_map/all_gather | solution.py:12
  7.3 299.5 %all-gather.6.cloned.1.call-start = ((), (), s32[]{:S(2)}) async-start(), calls=%async_computation.1 | async-start | bytes 42467328 | tf_op jit(solution)/shard_map/all_gather | solution.py:17
  8.0 480.3 %all-gather.8.cloned.1.call-start = ((), (), s32[]{:S(2)}) async-start(), calls=%async_computation.2 | async-start | bytes 42467328 | tf_op jit(solution)/shard_map/all_gather | solution.py:18
Sparse Core Ops, SparseCore 0:
  8.9 118.0 all-gather.3
  128.9 177.7 all-gather.5
  308.6 179.5 all-gather.7
where the time goes:
time: 524 us; the launch traced here: 523 us
  waiting for transfers between devices  454 us (87%)
  matrix products  56 us (11%)
  between operations  13.1 us (2%)
    all_gather x1, waiting for transfers between devices, per_device(): lax.all_gather(gate_weight, 'row', axis=0, tiled=True)  180 us
    all_gather x1, waiting for transfers between devices, per_device(): up_sum = add_single(lax.all_gather(up_weight, 'row', axis=0, tiled=True))  154 us
    all_gather x1, waiting for transfers between devices, per_device(): gathered = lax.all_gather(tokens, 'col', axis=1, tiled=True)  118 us
    dot_general x2, matrix products, accumulate(): return jnp.dot(gathered, weight_rows, preferred_element_type=jnp.float32)  56 us
  transfers between devices with their start and end apart: 3, of which 3 were waited for; matrix products, arithmetic and copies ran while one was open for 5% of the time, Pallas kernels for 0%

commit v1 on v0

v1 whole, which is shorter than its diff:
```python
import functools

import jax
import jax.numpy as jnp
from jax import lax
from jax.experimental import pallas as pl
from jax.experimental.pallas import tpu as pltpu
from jax.sharding import PartitionSpec as P

MESH = pl.DeviceIdType.MESH


def kernel(Y, X, Z, n, tok, gate, up, out, T, W, O, loc, sibs, sibr, tls, tlr, ts, tr, tfs, tfr,
           xs, xr, ys, yr, fas, far, fbs, fbr, ol, osd, orv, tl):
    rows, kz = tok.shape
    kr = gate.shape[0]
    half = gate.shape[1] // 2
    J = half // n
    row, z = lax.axis_index("row"), lax.axis_index("col")
    c, p = lax.rem(row, 2), row // 2
    x, y = lax.rem(p, X), p // X
    sib = row + 1 - 2 * c
    kc = 2 * kr

    def chip(yy, xx):
        return yy * X + xx

    def al(v, k):
        return pl.multiple_of(v, k)

    def remote(src, dst, s, r, drow, dcol):
        return pltpu.make_async_remote_copy(
            src_ref=src, dst_ref=dst, send_sem=s, recv_sem=r,
            device_id=(drow, dcol), device_id_type=MESH)

    def block(j, q):
        return W.at[j, pl.ds(al(q * kc, kc), kc), :]

    def part(j, q, h):
        return W.at[j, pl.ds(al(q * kc + h * kr, kr), kr), :]

    xpeers = [lax.rem(x + d, X) for d in range(1, X)]
    xfrom = [lax.rem(x + X - d, X) for d in range(1, X)]
    ypeers = [lax.rem(y + d, Y) for d in range(1, Y)]
    yfrom = [lax.rem(y + Y - d, Y) for d in range(1, Y)]
    zpeers = [lax.rem(z + d, Z) for d in range(1, Z)]
    zfrom = [lax.rem(z + Z - d, Z) for d in range(1, Z)]

    barrier = pltpu.get_barrier_semaphore()
    peers = [(sib, z)] + [(row, q) for q in zpeers]
    peers += [(chip(y, q) * 2 + c, z) for q in xpeers]
    peers += [(chip(q, x) * 2 + c, z) for q in ypeers]
    for q in peers:
        pl.semaphore_signal(barrier, inc=1, device_id=q, device_id_type=MESH)
    pl.semaphore_wait(barrier, len(peers))

    def local_copies(j):
        return [
            pltpu.make_async_copy(
                ref.at[:, pl.ds(al(c * half + j * n, n), n)],
                W.at[j, pl.ds(al(row * kr, kr), kr), pl.ds(i * n, n)],
                loc.at[j, i])
            for i, ref in enumerate((gate, up))]

    def sib_copies(j, owner, other):
        return [
            remote(
                ref.at[:, pl.ds(al(other * half + j * n, n), n)],
                W.at[j, pl.ds(al(owner * kr, kr), kr), pl.ds(i * n, n)],
                sibs.at[j, i], sibr.at[j, i], sib, z)
            for i, ref in enumerate((gate, up))]

    def fetch(j):
        for k in local_copies(j) + sib_copies(j, row, 1 - c):
            k.start()

    def xdirect(j, d, q):
        return remote(block(j, q), block(j, q), xs.at[j, d], xr.at[j, d],
                      chip(y, xpeers[d]) * 2 + c, z)

    def ydirect(j, d, q):
        return remote(block(j, q), block(j, q), ys.at[j, d], yr.at[j, d],
                      chip(ypeers[d], x) * 2 + c, z)

    def fwda(j, dx, dy, q):
        return remote(part(j, q, 0), part(j, q, 0), fas.at[j, dx, dy], far.at[j, dx, dy],
                      chip(ypeers[dy], x) * 2 + c, z)

    def fwdb(j, dx, dy, q):
        return remote(part(j, q, 1), part(j, q, 1), fbs.at[j, dx, dy], fbr.at[j, dx, dy],
                      chip(y, xpeers[dx]) * 2 + c, z)

    def trows(q, core):
        return T.at[q, pl.ds(al(core * rows, rows), rows), :]

    tok_local = pltpu.make_async_copy(tok, trows(z, c), tl.at[0])
    tok_sib = remote(tok, trows(z, c), tls.at[0], tlr.at[0], sib, z)
    tok_send = [remote(tok, trows(z, c), ts.at[d], tr.at[d], row, zpeers[d]) for d in range(Z - 1)]

    def tok_fwd(d, core):
        return remote(trows(zfrom[d], core), trows(zfrom[d], core), tfs.at[d], tfr.at[d], sib, z)

    def out_local(j):
        return pltpu.make_async_copy(
            O.at[j, pl.ds(al(c * rows, rows), rows), :],
            out.at[:, pl.ds(al(c * half + j * n, n), n)], ol.at[j])

    def out_sib(j, core):
        return remote(
            O.at[j, pl.ds(al((1 - c) * rows, rows), rows), :],
            out.at[:, pl.ds(al(core * half + j * n, n), n)], osd.at[j], orv.at[j], sib, z)

    fetch(0)
    for k in tok_send:
        k.start()
    if J > 1:
        fetch(1)
    tok_local.start()
    tok_sib.start()

    late = (J + 1) // 2

    def done(s):
        return jnp.maximum(jnp.minimum(s - 1, 2 * (s - late + 1)), 0)

    def compute(j, carry):
        for d in range(X - 1):
            for e in range(Y - 1):
                q = chip(yfrom[e], xfrom[d])
                fwda(j, d, e, q).wait_recv()
                fwdb(j, d, e, q).wait_recv()

        def tile(m, carry):
            r = pl.ds(al(m * rows, rows), rows)
            total = jnp.zeros((rows, 2 * n), jnp.float32)
            for q in range(Z):
                total += jnp.dot(T[q, r, :], W[j, q * kz:(q + 1) * kz, :],
                                 preferred_element_type=jnp.float32)
            g, u = total[:, :n], total[:, n:]
            O[j, r, :] = g / (1.0 + jnp.exp(-g)) * u
            return carry

        lax.fori_loop(0, 2, tile, 0)
        out_local(j).start()
        out_sib(j, c).start()
        return carry

    def step(s, carry):
        @pl.when(s < J)
        def _():
            for k in local_copies(s):
                k.wait()
            for k in sib_copies(s, sib, 1 - c):
                k.wait_recv()
            for d in range(X - 1):
                xdirect(s, d, p).start()
            for d in range(Y - 1):
                ydirect(s, d, p).start()

        @pl.when(s + 2 < J)
        def _():
            fetch(s + 2)

        @pl.when(jnp.logical_and(s >= 1, s <= J))
        def _():
            j = s - 1
            for d in range(X - 1):
                q = chip(y, xfrom[d])
                xdirect(j, d, q).wait_recv()
                for e in range(Y - 1):
                    fwda(j, d, e, q).start()
            for e in range(Y - 1):
                q = chip(yfrom[e], x)
                ydirect(j, e, q).wait_recv()
                for d in range(X - 1):
                    fwdb(j, d, e, q).start()

        @pl.when(s == late - 1)
        def _():
            for d in range(Z - 1):
                tok_send[d].wait_recv()
                tok_fwd(d, c).start()

        @pl.when(s == late)
        def _():
            tok_local.wait()
            remote(tok, trows(z, 1 - c), tls.at[0], tlr.at[0], sib, z).wait_recv()
            for d in range(Z - 1):
                tok_fwd(d, 1 - c).wait_recv()

        lax.fori_loop(done(s - 1), done(s), compute, 0)
        return carry

    lax.fori_loop(0, J + 2, step, 0)

    tok_sib.wait_send()
    for d in range(Z - 1):
        tok_send[d].wait_send()
        tok_fwd(d, c).wait_send()

    def finish(j, carry):
        for k in sib_copies(j, row, 1 - c):
            k.wait_send()
        for d in range(X - 1):
            xdirect(j, d, p).wait_send()
            for e in range(Y - 1):
                fwda(j, d, e, chip(y, xfrom[d])).wait_send()
        for e in range(Y - 1):
            ydirect(j, e, p).wait_send()
            for d in range(X - 1):
                fwdb(j, d, e, chip(yfrom[e], x)).wait_send()
        out_local(j).wait()
        out_sib(j, c).wait_send()
        out_sib(j, 1 - c).wait_recv()
        return carry

    lax.fori_loop(0, J, finish, 0)


def solution(mesh):
    R, Z = mesh.shape["row"], mesh.shape["col"]
    chips = R // 2
    Y = 2 if chips % 2 == 0 else 1
    X = chips // Y

    def per_device(tokens, gate_weight, up_weight):
        rows, kz = tokens.shape
        kr, cols = gate_weight.shape
        n = 128
        half = cols // 2
        J = half // n
        dma = pltpu.SemaphoreType.DMA
        ux, uy, uz = max(X - 1, 1), max(Y - 1, 1), max(Z - 1, 1)
        scratch = [
            pltpu.VMEM((Z, 2 * rows, kz), jnp.bfloat16),
            pltpu.VMEM((J, R * kr, 2 * n), jnp.bfloat16),
            pltpu.VMEM((J, 2 * rows, n), jnp.float32),
            dma((J, 2)), dma((J, 2)), dma((J, 2)),
            dma((1,)), dma((1,)), dma((uz,)), dma((uz,)), dma((uz,)), dma((uz,)),
            dma((J, ux)), dma((J, ux)), dma((J, uy)), dma((J, uy)),
            dma((J, ux, uy)), dma((J, ux, uy)), dma((J, ux, uy)), dma((J, ux, uy)),
            dma((J,)), dma((J,)), dma((J,)), dma((1,)),
        ]
        return pl.pallas_call(
            functools.partial(kernel, Y, X, Z, n),
            out_shape=jax.ShapeDtypeStruct((rows, cols), jnp.float32),
            in_specs=[pl.BlockSpec(memory_space=pl.ANY)] * 3,
            out_specs=pl.BlockSpec(memory_space=pl.ANY),
            scratch_shapes=scratch,
            compiler_params=pltpu.CompilerParams(
                collective_id=0, has_side_effects=True, vmem_limit_bytes=62 * 2**20),
            cost_estimate=pl.CostEstimate(
                flops=4 * rows * R * kr * cols, bytes_accessed=4 * rows * cols,
                transcendentals=rows * cols),
        )(tokens, gate_weight, up_weight)

    return jax.shard_map(
        per_device, mesh=mesh, in_specs=(P("row", "col"),) * 3,
        out_specs=P("row", "col"), check_vma=False)
```

time: 524 us -> 326 us (0.62)
  waiting for transfers between devices: 454 us -> 0 us
  Pallas kernels: 0 us -> 319 us
  matrix products: 56 us -> 0 us
  between operations: 13.1 us -> 0.01 us
  local copies, waits for them, and re-layouts: 0 us -> 6.23 us
    all_gather x3 -> x0, waiting for transfers between devices: 452 us -> none  [the longest x1 180 us: per_device(): lax.all_gather(gate_weight, 'row', axis=0, tiled=True)]
    pallas_call x0 -> x1, Pallas kernels: none -> 319 us  [per_device(): pl.pallas_call(functools.partial(kernel, Y, X, Z, n), out_shape=jax.Shape...]
    dot_general x2 -> x0, matrix products: 56 us -> none  [accumulate(): return jnp.dot(gathered, weight_rows, preferred_element_type=jnp.float32)]
    unnamed x0 -> x1, local copies, waits for them, and re-layouts: none -> 6.23 us
  transfers between devices with their start and end apart: 3 -> 0, of which waited for: 3 -> 0; matrix products, arithmetic and copies ran while one was open for 5% -> 0% of each run, Pallas kernels for 0% -> 0%
where the time goes in v1:
time: 326 us; the launch traced here: 325 us
  Pallas kernels  319 us (98%)
  local copies, waits for them, and re-layouts  6.23 us (2%)
    pallas_call x1, Pallas kernels, per_device(): pl.pallas_call(functools.partial(kernel, Y, X, Z, n), out_shape=jax.Shape...  319 us

profile of v1, /device:TPU:0, one launch (start us, length us, event | category | flops | bytes accessed | tf_op | source)
XLA Modules:
  0.0 325.4 jit_solution(13714779957564451246)
XLA Ops:
  0.0 319.1 %shard_map.37 = f32[512,3072]{1,0:T(8,128)} custom-call(bf16[512,1536]{1,0:T(8,128)(2,1)} %tok.1, bf16[768,3072]{1,0:T(8,128)(2,1)} %gate.1, bf16[768,3072]{1,0:T(8,128)(2,1)} %up.1), custom_call_target="tpu_custom_call" | custom-call | flops 38654705664 | bytes 6291456 | tf_op jit(solution)/shard_map/pallas_call | solution.py:244
  319.1 6.2 %copy.5 = f32[512,3072]{1,0:T(8,128)} copy(f32[512,3072]{1,0:T(8,128)} %shard_map.37) | data formatting | bytes 12582912

commit v2 on v1

--- a/solution.py
+++ b/solution.py
@@ -217,6 +217,276 @@
     lax.fori_loop(0, J, finish, 0)
 
 
+def grid_kernel(Y, X, Z, n, tok, gate, up, out, T, W, O, loc, sibs, sibr, ys, yr, xs, xr,
+                tl, hs, hr, zs, zr, fs, fr, ol, osd, orv):
+    rows, kz = tok.shape
+    kr = gate.shape[0]
+    quarter = gate.shape[1] // 4
+    J = quarter // n
+    kc = 2 * kr
+    row, z = lax.axis_index("row"), lax.axis_index("col")
+    c, p = lax.rem(row, 2), row // 2
+    x, y = lax.rem(p, X), p // X
+    c2, y2 = 1 - c, 1 - y
+
+    def dev(yy, xx, cc):
+        return (yy * X + xx) * 2 + cc
+
+    def al(v, k):
+        return pl.multiple_of(v, k)
+
+    def remote(src, dst, s, r, drow, dcol):
+        return pltpu.make_async_remote_copy(
+            src_ref=src, dst_ref=dst, send_sem=s, recv_sem=r,
+            device_id=(drow, dcol), device_id_type=MESH)
+
+    sib, across, cross = dev(y, x, c2), dev(y2, x, c), dev(y2, x, c2)
+    xpeers = [lax.rem(x + d, X) for d in range(1, X)]
+    xfrom = [lax.rem(x + X - d, X) for d in range(1, X)]
+
+    barrier = pltpu.get_barrier_semaphore()
+
+    def greet(drow, dcol):
+        pl.semaphore_signal(barrier, inc=1, device_id=(drow, dcol), device_id_type=MESH)
+
+    for q in [sib, across, cross] + [dev(y, q, c) for q in xpeers]:
+        greet(q, z)
+
+    @pl.when(z > 0)
+    def _():
+        greet(row, z - 1)
+
+    @pl.when(z < Z - 1)
+    def _():
+        greet(row, z + 1)
+
+    pl.semaphore_wait(barrier, 2 + X + jnp.minimum(z, 1) + jnp.minimum(Z - 1 - z, 1))
+
+    def cols(ref, yy, cc, j):
+        return ref.at[:, pl.ds(al((yy * 2 + cc) * quarter + j * n, n), n)]
+
+    def place(j, owner, i):
+        return W.at[j, pl.ds(al(owner * kr, kr), kr), pl.ds(i * n, n)]
+
+    def local_copies(j):
+        return [pltpu.make_async_copy(cols(ref, y, c, j), place(j, row, i), loc.at[j, i])
+                for i, ref in enumerate((gate, up))]
+
+    def sib_copies(j, owner):
+        return [remote(cols(ref, y, c2, j), place(j, owner, i), sibs.at[j, i], sibr.at[j, i], sib, z)
+                for i, ref in enumerate((gate, up))]
+
+    def y_copies(j, owners):
+        return [remote(cols(ref, y2, cc, j), place(j, owners[k], i), ys.at[j, k, i], yr.at[j, k, i],
+                       dest, z)
+                for k, (cc, dest) in enumerate(((c, across), (c2, cross)))
+                for i, ref in enumerate((gate, up))]
+
+    def x_copy(j, d, k, q):
+        yy = y2 if k else y
+        b = W.at[j, pl.ds(al((yy * X + q) * kc, kc), kc), :]
+        return remote(b, b, xs.at[j, d, k], xr.at[j, d, k], dev(y, xpeers[d], c), z)
+
+    def fetch(j):
+        for k in local_copies(j) + sib_copies(j, row) + y_copies(j, (row, row)):
+            k.start()
+
+    def trows(q, t, core):
+        return T.at[q, pl.ds(al(((y if t else y2) * 2 + core) * rows, rows), rows), :]
+
+    tok_local = pltpu.make_async_copy(tok, trows(z, 1, c), tl.at[0])
+    tok_y = remote(tok, trows(z, 1, c), hs.at[0], hr.at[0], across, z)
+    tok_y_in = remote(tok, trows(z, 0, c), hs.at[0], hr.at[0], across, z)
+    tok_sib = remote(tok, trows(z, 1, c), hs.at[1], hr.at[1], sib, z)
+    tok_sib_in = remote(tok, trows(z, 1, c2), hs.at[1], hr.at[1], sib, z)
+
+    def pair_sib(core):
+        return remote(trows(z, 0, core), trows(z, 0, core), hs.at[2], hr.at[2], sib, z)
+
+    def hop(t, h, up_way, q):
+        w = 0 if up_way else 1
+        dst = z + 1 if up_way else z - 1
+        src = tok if (t == 1 and h == 1) else trows(q, t, c)
+        return remote(src, trows(q, t, c), zs.at[t, h - 1, w], zr.at[t, h - 1, w], row, dst)
+
+    def has_send(h, up_way):
+        return (jnp.logical_and(z >= h - 1, z < Z - 1) if up_way
+                else jnp.logical_and(z <= Z - h, z > 0))
+
+    def has_recv(h, up_way):
+        return z >= h if up_way else z < Z - h
+
+    def hop_send(t, h, wait=False):
+        for up_way in (True, False):
+            @pl.when(has_send(h, up_way))
+            def _():
+                q = z - (h - 1) if up_way else z + (h - 1)
+                k = hop(t, h, up_way, q)
+                if wait:
+                    k.wait_send()
+                else:
+                    k.start()
+
+    def to_sib(t, h, up_way, core):
+        q = z - h if up_way else z + h
+        w = 0 if up_way else 1
+        return remote(trows(q, t, core), trows(q, t, core), fs.at[t, h - 1, w], fr.at[t, h - 1, w], sib, z)
+
+    def hop_recv(t, h):
+        for up_way in (True, False):
+            @pl.when(has_recv(h, up_way))
+            def _():
+                q = z - h if up_way else z + h
+                hop(t, h, up_way, q).wait_recv()
+                to_sib(t, h, up_way, c).start()
+
+            if h < Z - 1:
+                @pl.when(has_send(h + 1, up_way))
+                def _():
+                    hop(t, h + 1, up_way, z - h if up_way else z + h).start()
+
+    def sib_wait(t, send):
+        for h in range(1, Z):
+            for up_way in (True, False):
+                @pl.when(has_recv(h, up_way))
+                def _():
+                    if send:
+                        to_sib(t, h, up_way, c).wait_send()
+                    else:
+                        to_sib(t, h, up_way, c2).wait_recv()
+
+    def orows(j, yy, cc):
+        return O.at[j, pl.ds(al((yy * 2 + cc) * rows, rows), rows), :]
+
+    def out_local(j):
+        return pltpu.make_async_copy(orows(j, y, c), cols(out, y, c, j), ol.at[j])
+
+    def out_copy(j, k, incoming=False):
+        yy, cc, dest = ((y, c2, sib), (y2, c, across), (y2, c2, cross))[k]
+        fy, fc = (yy, cc) if incoming else (y, c)
+        return remote(orows(j, yy, cc), cols(out, fy, fc, j), osd.at[j, k], orv.at[j, k], dest, z)
+
+    def tiles(j, yy):
+        def tile(m, carry):
+            r = pl.ds(al((yy * 2 + m) * rows, rows), rows)
+            total = jnp.zeros((rows, 2 * n), jnp.float32)
+            for q in range(Z):
+                total += jnp.dot(T[q, r, :], W[j, q * kz:(q + 1) * kz, :],
+                                 preferred_element_type=jnp.float32)
+            g, u = total[:, :n], total[:, n:]
+            O[j, r, :] = g / (1.0 + jnp.exp(-g)) * u
+            return carry
+
+        lax.fori_loop(0, 2, tile, 0)
+
+    def compute_pair(j, carry):
+        tiles(j, y2)
+        out_copy(j, 1).start()
+        out_copy(j, 2).start()
+        return carry
+
+    def compute_own(j, carry):
+        tiles(j, y)
+        out_local(j).start()
+        out_copy(j, 0).start()
+        return carry
+
+    tok_y.start()
+    fetch(0)
+    tok_local.start()
+    tok_sib.start()
+    fetch(1)
+
+    def done(s):
+        return jnp.where(s < Z - 1, 0, s)
+
+    def step(s, carry):
+        @pl.when(s < J)
+        def _():
+            for k in local_copies(s):
+                k.wait()
+            for k in sib_copies(s, sib):
+                k.wait_recv()
+            for d in range(X - 1):
+                x_copy(s, d, 0, x).start()
+
+        @pl.when(s + 2 < J)
+        def _():
+            fetch(s + 2)
+
+        @pl.when(s == 0)
+        def _():
+            tok_y_in.wait_recv()
+            hop_send(0, 1)
+            pair_sib(c).start()
+
+        @pl.when(s < J)
+        def _():
+            for k in y_copies(s, (across, cross)):
+                k.wait_recv()
+            for d in range(X - 1):
+                x_copy(s, d, 1, x).start()
+
+        for h in range(1, Z):
+            @pl.when(s == h)
+            def _():
+                hop_recv(0, h)
+                if h == max(Z - 2, 1):
+                    hop_send(1, 1)
+
+        for h in range(1, Z):
+            @pl.when(s == (J if h == Z - 1 else Z - 2 + h))
+            def _():
+                hop_recv(1, h)
+
+        @pl.when(s == Z - 1)
+        def _():
+            pair_sib(c2).wait_recv()
+            sib_wait(0, False)
+
+        @pl.when(s == J)
+        def _():
+            tok_local.wait()
+            tok_sib_in.wait_recv()
+            sib_wait(1, False)
+
+        lax.fori_loop(0, jnp.where(s == J, J - 1, 0), compute_own, 0)
+
+        @pl.when(s >= 1)
+        def _():
+            for d in range(X - 1):
+                for k in range(2):
+                    x_copy(s - 1, d, k, xfrom[d]).wait_recv()
+
+        lax.fori_loop(done(s - 1), done(s), compute_pair, 0)
+        return carry
+
+    lax.fori_loop(0, J + 1, step, 0)
+    compute_own(J - 1, 0)
+
+    tok_y.wait_send()
+    tok_sib.wait_send()
+    pair_sib(c).wait_send()
+    for t in range(2):
+        sib_wait(t, True)
+        for h in range(1, Z):
+            hop_send(t, h, wait=True)
+
+    def finish(j, carry):
+        for k in sib_copies(j, row) + y_copies(j, (row, row)):
+            k.wait_send()
+        for d in range(X - 1):
+            for k in range(2):
+                x_copy(j, d, k, x).wait_send()
+        out_local(j).wait()
+        for k in range(3):
+            out_copy(j, k).wait_send()
+            out_copy(j, k, True).wait_recv()
+        return carry
+
+    lax.fori_loop(0, J, finish, 0)
+
+
 def solution(mesh):
     R, Z = mesh.shape["row"], mesh.shape["col"]
     chips = R // 2
@@ -231,6 +501,8 @@
         J = half // n
         dma = pltpu.SemaphoreType.DMA
         ux, uy, uz = max(X - 1, 1), max(Y - 1, 1), max(Z - 1, 1)
+        quarter = cols // 4
+        grid = Y == 2 and Z > 2 and quarter % n == 0 and quarter // n >= 2 * Z - 2
         scratch = [
             pltpu.VMEM((Z, 2 * rows, kz), jnp.bfloat16),
             pltpu.VMEM((J, R * kr, 2 * n), jnp.bfloat16),
@@ -241,8 +513,19 @@
             dma((J, ux, uy)), dma((J, ux, uy)), dma((J, ux, uy)), dma((J, ux, uy)),
             dma((J,)), dma((J,)), dma((J,)), dma((1,)),
         ]
+        if grid:
+            J = quarter // n
+            scratch = [
+                pltpu.VMEM((Z, 4 * rows, kz), jnp.bfloat16),
+                pltpu.VMEM((J, R * kr, 2 * n), jnp.bfloat16),
+                pltpu.VMEM((J, 4 * rows, n), jnp.float32),
+                dma((J, 2)), dma((J, 2)), dma((J, 2)), dma((J, 2, 2)), dma((J, 2, 2)),
+                dma((J, ux, 2)), dma((J, ux, 2)), dma((1,)), dma((3,)), dma((3,)),
+                dma((2, uz, 2)), dma((2, uz, 2)), dma((2, uz, 2)), dma((2, uz, 2)),
+                dma((J,)), dma((J, 3)), dma((J, 3)),
+            ]
         return pl.pallas_call(
-            functools.partial(kernel, Y, X, Z, n),
+            functools.partial(grid_kernel if grid else kernel, Y, X, Z, n),
             out_shape=jax.ShapeDtypeStruct((rows, cols), jnp.float32),
             in_specs=[pl.BlockSpec(memory_space=pl.ANY)] * 3,
             out_specs=pl.BlockSpec(memory_space=pl.ANY),

time: 326 us -> 290 us (0.89)
  Pallas kernels: 319 us -> 283 us
    pallas_call x1, Pallas kernels: 319 us -> 283 us  [per_device(): pl.pallas_call(functools.partial(grid_kernel if grid else kernel, Y, X, Z...]
where the time goes in v2:
time: 290 us; the launch traced here: 289 us
  Pallas kernels  283 us (98%)
  local copies, waits for them, and re-layouts  6.23 us (2%)
    pallas_call x1, Pallas kernels, per_device(): pl.pallas_call(functools.partial(grid_kernel if grid else kernel, Y, X, Z...  283 us
    unnamed x1, local copies, waits for them, and re-layouts  6.23 us

profile of v2, /device:TPU:0, one launch (start us, length us, event | category | flops | bytes accessed | tf_op | source)
XLA Modules:
  0.0 289.4 jit_solution(12947816067525132859)
XLA Ops:
  0.0 283.2 %shard_map.37 = f32[512,3072]{1,0:T(8,128)} custom-call(bf16[512,1536]{1,0:T(8,128)(2,1)} %tok.1, bf16[768,3072]{1,0:T(8,128)(2,1)} %gate.1, bf16[768,3072]{1,0:T(8,128)(2,1)} %up.1), custom_call_target="tpu_custom_call" | custom-call | flops 38654705664 | bytes 6291456 | tf_op jit(solution)/shard_map/pallas_call | solution.py:527
  283.2 6.2 %copy.5 = f32[512,3072]{1,0:T(8,128)} copy(f32[512,3072]{1,0:T(8,128)} %shard_map.37) | data formatting | bytes 12582912

commit v3 on v2

--- a/solution.py
+++ b/solution.py
@@ -217,7 +217,7 @@
     lax.fori_loop(0, J, finish, 0)
 
 
-def grid_kernel(Y, X, Z, n, tok, gate, up, out, T, W, O, loc, sibs, sibr, ys, yr, xs, xr,
+def grid_kernel(Y, X, Z, n, tok, gate, up, out, T, W, O, U, loc, sibs, sibr, ys, yr, xs, xr,
                 tl, hs, hr, zs, zr, fs, fr, ol, osd, orv):
     rows, kz = tok.shape
     kr = gate.shape[0]
@@ -288,7 +288,11 @@
         return remote(b, b, xs.at[j, d, k], xr.at[j, d, k], dev(y, xpeers[d], c), z)
 
     def fetch(j):
-        for k in local_copies(j) + sib_copies(j, row) + y_copies(j, (row, row)):
+        for k in local_copies(j) + sib_copies(j, row):
+            k.start()
+
+    def fetch_y(j):
+        for k in y_copies(j, (row, row)):
             k.start()
 
     def trows(q, t, core):
@@ -345,8 +349,8 @@
                 def _():
                     hop(t, h + 1, up_way, z - h if up_way else z + h).start()
 
-    def sib_wait(t, send):
-        for h in range(1, Z):
+    def sib_wait(t, send, first, last):
+        for h in range(first, last + 1):
             for up_way in (True, False):
                 @pl.when(has_recv(h, up_way))
                 def _():
@@ -379,46 +383,85 @@
 
         lax.fori_loop(0, 2, tile, 0)
 
+    far_z = jnp.where(z < Z // 2, Z - 1, 0)
+    near_first = jnp.where(z < Z // 2, 0, 1)
+
+    def slab(j, r, q):
+        return jnp.dot(T[q, r, :], W[j, pl.ds(al(q * kz, kz), kz), :],
+                       preferred_element_type=jnp.float32)
+
+    def own_near(j, carry):
+        def tile(m, carry):
+            r = pl.ds(al((y * 2 + m) * rows, rows), rows)
+            total = slab(j, r, near_first)
+            for i in range(1, Z - 1):
+                total += slab(j, r, near_first + i)
+            O[j, r, :] = total[:, :n]
+            U[j, pl.ds(al(m * rows, rows), rows), :] = total[:, n:]
+            return carry
+
+        lax.fori_loop(0, 2, tile, 0)
+        return carry
+
+    def own_far(j, carry):
+        def tile(m, carry):
+            r = pl.ds(al((y * 2 + m) * rows, rows), rows)
+            total = slab(j, r, far_z)
+            g = O[j, r, :] + total[:, :n]
+            u = U[j, pl.ds(al(m * rows, rows), rows), :] + total[:, n:]
+            O[j, r, :] = g / (1.0 + jnp.exp(-g)) * u
+            return carry
+
+        lax.fori_loop(0, 2, tile, 0)
+        out_local(j).start()
+        out_copy(j, 0).start()
+        return carry
+
     def compute_pair(j, carry):
         tiles(j, y2)
         out_copy(j, 1).start()
         out_copy(j, 2).start()
         return carry
 
-    def compute_own(j, carry):
-        tiles(j, y)
-        out_local(j).start()
-        out_copy(j, 0).start()
-        return carry
-
+    lead = min(3, J)
     tok_y.start()
+    hop_send(1, 1)
     fetch(0)
+    fetch_y(0)
     tok_local.start()
     tok_sib.start()
-    fetch(1)
+    for j in range(1, lead):
+        fetch(j)
 
     def done(s):
         return jnp.where(s < Z - 1, 0, s)
 
+    def send_own(j, carry):
+        for k in local_copies(j):
+            k.wait()
+        for k in sib_copies(j, sib):
+            k.wait_recv()
+        for d in range(X - 1):
+            x_copy(j, d, 0, x).start()
+        return carry
+
     def step(s, carry):
-        @pl.when(s < J)
-        def _():
-            for k in local_copies(s):
-                k.wait()
-            for k in sib_copies(s, sib):
-                k.wait_recv()
-            for d in range(X - 1):
-                x_copy(s, d, 0, x).start()
-
-        @pl.when(s + 2 < J)
-        def _():
-            fetch(s + 2)
+        lax.fori_loop(jnp.where(s == 0, 0, s + lead - 1), jnp.minimum(s + lead, J), send_own, 0)
+
+        @pl.when(s + lead < J)
+        def _():
+            fetch(s + lead)
 
         @pl.when(s == 0)
         def _():
             tok_y_in.wait_recv()
             hop_send(0, 1)
             pair_sib(c).start()
+            fetch_y(1)
+
+        @pl.when(s + 2 < J)
+        def _():
+            fetch_y(s + 2)
 
         @pl.when(s < J)
         def _():
@@ -431,26 +474,18 @@
             @pl.when(s == h)
             def _():
                 hop_recv(0, h)
-                if h == max(Z - 2, 1):
-                    hop_send(1, 1)
-
-        for h in range(1, Z):
-            @pl.when(s == (J if h == Z - 1 else Z - 2 + h))
+
+        for h in range(1, Z - 1):
+            @pl.when(s == Z - 2 + h)
             def _():
                 hop_recv(1, h)
 
         @pl.when(s == Z - 1)
         def _():
             pair_sib(c2).wait_recv()
-            sib_wait(0, False)
-
-        @pl.when(s == J)
-        def _():
-            tok_local.wait()
-            tok_sib_in.wait_recv()
-            sib_wait(1, False)
-
-        lax.fori_loop(0, jnp.where(s == J, J - 1, 0), compute_own, 0)
+            sib_wait(0, False, 1, Z - 1)
+
+        lax.fori_loop(jnp.where(s == J, J - 2, 0), jnp.where(s == J, J - 1, 0), own_near, 0)
 
         @pl.when(s >= 1)
         def _():
@@ -459,16 +494,30 @@
                     x_copy(s - 1, d, k, xfrom[d]).wait_recv()
 
         lax.fori_loop(done(s - 1), done(s), compute_pair, 0)
+
+        @pl.when(s == J - 1)
+        def _():
+            tok_local.wait()
+            tok_sib_in.wait_recv()
+            sib_wait(1, False, 1, Z - 2)
+
+        @pl.when(s == J)
+        def _():
+            hop_recv(1, Z - 1)
+
+        lax.fori_loop(jnp.where(s == J, J - 1, 0), jnp.where(s == J, J, jnp.where(s == J - 1, J - 2, 0)),
+                      own_near, 0)
         return carry
 
     lax.fori_loop(0, J + 1, step, 0)
-    compute_own(J - 1, 0)
+    sib_wait(1, False, Z - 1, Z - 1)
+    lax.fori_loop(0, J, own_far, 0)
 
     tok_y.wait_send()
     tok_sib.wait_send()
     pair_sib(c).wait_send()
     for t in range(2):
-        sib_wait(t, True)
+        sib_wait(t, True, 1, Z - 1)
         for h in range(1, Z):
             hop_send(t, h, wait=True)
 
@@ -519,6 +568,7 @@
                 pltpu.VMEM((Z, 4 * rows, kz), jnp.bfloat16),
                 pltpu.VMEM((J, R * kr, 2 * n), jnp.bfloat16),
                 pltpu.VMEM((J, 4 * rows, n), jnp.float32),
+                pltpu.VMEM((J, 2 * rows, n), jnp.float32),
                 dma((J, 2)), dma((J, 2)), dma((J, 2)), dma((J, 2, 2)), dma((J, 2, 2)),
                 dma((J, ux, 2)), dma((J, ux, 2)), dma((1,)), dma((3,)), dma((3,)),
                 dma((2, uz, 2)), dma((2, uz, 2)), dma((2, uz, 2)), dma((2, uz, 2)),

time: 290 us -> 236 us (0.81)
  Pallas kernels: 283 us -> 230 us
    pallas_call x1, Pallas kernels: 283 us -> 230 us  [per_device(): pl.pallas_call(functools.partial(grid_kernel if grid else kernel, Y, X, Z...]
where the time goes in v3:
time: 236 us
  Pallas kernels  230 us (97%)
  local copies, waits for them, and re-layouts  6.23 us (3%)
    pallas_call x1, Pallas kernels, per_device(): pl.pallas_call(functools.partial(grid_kernel if grid else kernel, Y, X, Z...  230 us
    unnamed x1, local copies, waits for them, and re-layouts  6.23 us

profile of v3, /device:TPU:0, one launch (start us, length us, event | category | flops | bytes accessed | tf_op | source)
XLA Modules:
  0.0 236.0 jit_solution(10008937953447422703)
XLA Ops:
  0.0 229.7 %shard_map.37 = f32[512,3072]{1,0:T(8,128)} custom-call(bf16[512,1536]{1,0:T(8,128)(2,1)} %tok.1, bf16[768,3072]{1,0:T(8,128)(2,1)} %gate.1, bf16[768,3072]{1,0:T(8,128)(2,1)} %up.1), custom_call_target="tpu_custom_call" | custom-call | flops 38654705664 | bytes 6291456 | tf_op jit(solution)/shard_map/pallas_call | solution.py:577
  229.8 6.2 %copy.5 = f32[512,3072]{1,0:T(8,128)} copy(f32[512,3072]{1,0:T(8,128)} %shard_map.37) | data formatting | bytes 12582912

commit v4 on v3

--- a/solution.py
+++ b/solution.py
@@ -423,6 +423,25 @@
         out_copy(j, 2).start()
         return carry
 
+    split = X == 2 and Z == X * Y
+    early = [y * X + x, y2 * X + x, y * X + xfrom[0]]
+
+    def last_near(m, carry):
+        r = pl.ds(al((y2 * 2 + m) * rows, rows), rows)
+        total = slab(J - 1, r, early[0])
+        for q in early[1:]:
+            total += slab(J - 1, r, q)
+        O[J - 1, r, :] = total[:, :n]
+        U[J, pl.ds(al(m * rows, rows), rows), :] = total[:, n:]
+        return carry
+
+    def last_far(m):
+        r = pl.ds(al((y2 * 2 + m) * rows, rows), rows)
+        total = slab(J - 1, r, y2 * X + xfrom[0])
+        g = O[J - 1, r, :] + total[:, :n]
+        u = U[J, pl.ds(al(m * rows, rows), rows), :] + total[:, n:]
+        O[J - 1, r, :] = g / (1.0 + jnp.exp(-g)) * u
+
     lead = min(3, J)
     tok_y.start()
     hop_send(1, 1)
@@ -490,10 +509,25 @@
         @pl.when(s >= 1)
         def _():
             for d in range(X - 1):
-                for k in range(2):
-                    x_copy(s - 1, d, k, xfrom[d]).wait_recv()
-
-        lax.fori_loop(done(s - 1), done(s), compute_pair, 0)
+                x_copy(s - 1, d, 0, xfrom[d]).wait_recv()
+
+        if split:
+            lax.fori_loop(0, jnp.where(s == J, 2, 0), last_near, 0)
+
+        @pl.when(s >= 1)
+        def _():
+            for d in range(X - 1):
+                x_copy(s - 1, d, 1, xfrom[d]).wait_recv()
+
+        if split:
+            @pl.when(s == J)
+            def _():
+                last_far(c)
+                out_copy(J - 1, 1).start()
+                last_far(c2)
+                out_copy(J - 1, 2).start()
+
+        lax.fori_loop(done(s - 1), jnp.minimum(done(s), J - 1 if split else J), compute_pair, 0)
 
         @pl.when(s == J - 1)
         def _():
@@ -568,7 +602,7 @@
                 pltpu.VMEM((Z, 4 * rows, kz), jnp.bfloat16),
                 pltpu.VMEM((J, R * kr, 2 * n), jnp.bfloat16),
                 pltpu.VMEM((J, 4 * rows, n), jnp.float32),
-                pltpu.VMEM((J, 2 * rows, n), jnp.float32),
+                pltpu.VMEM((J + 1, 2 * rows, n), jnp.float32),
                 dma((J, 2)), dma((J, 2)), dma((J, 2)), dma((J, 2, 2)), dma((J, 2, 2)),
                 dma((J, ux, 2)), dma((J, ux, 2)), dma((1,)), dma((3,)), dma((3,)),
                 dma((2, uz, 2)), dma((2, uz, 2)), dma((2, uz, 2)), dma((2, uz, 2)),

time: 236 us -> 237 us (level)
  no operation moved by 1% of the time
where the time goes in v4:
time: 237 us; the launch traced here: 236 us
  Pallas kernels  230 us (97%)
  local copies, waits for them, and re-layouts  6.23 us (3%)
    pallas_call x1, Pallas kernels, per_device(): pl.pallas_call(functools.partial(grid_kernel if grid else kernel, Y, X, Z...  230 us
    unnamed x1, local copies, waits for them, and re-layouts  6.23 us

profile of v4, /device:TPU:0, one launch (start us, length us, event | category | flops | bytes accessed | tf_op | source)
XLA Modules:
  0.0 236.4 jit_solution(3721774861294695166)
XLA Ops:
  0.0 230.2 %shard_map.37 = f32[512,3072]{1,0:T(8,128)} custom-call(bf16[512,1536]{1,0:T(8,128)(2,1)} %tok.1, bf16[768,3072]{1,0:T(8,128)(2,1)} %gate.1, bf16[768,3072]{1,0:T(8,128)(2,1)} %up.1), custom_call_target="tpu_custom_call" | custom-call | flops 38654705664 | bytes 6291456 | tf_op jit(solution)/shard_map/pallas_call | solution.py:611
  230.2 6.2 %copy.5 = f32[512,3072]{1,0:T(8,128)} copy(f32[512,3072]{1,0:T(8,128)} %shard_map.37) | data formatting | bytes 12582912
